TPU v7x, 32 devices: a whole 2x2x4 slice. The times are simulated.
32 devices in a mesh: dp: 16 (over z, y, x), outer: 2 (over core).
Axes of the slice: x: 2, y: 2, z: 4, core: 2. Of those that a mesh axis runs over, the one named last changes fastest.
Arguments:
- input_big: bfloat16 [64, 14, 14, 1024], P(('dp', 'outer'))
- input_small: bfloat16 [64, 10, 10, 1024], P(('dp', 'outer'))
- views_big: int32 [64], P(('dp', 'outer')), may hold values from 0 to 1, as said below
- views_small: int32 [64], P(('dp', 'outer')), may hold values from 0 to 1, as said below
- cotan_big: bfloat16 [64, 7, 7, 2048], P(('dp', 'outer'))
- cotan_small: bfloat16 [64, 5, 5, 2048], P(('dp', 'outer'))
- narrow_filter: bfloat16 [1024, 256], P('dp'), may hold values from -0.1875 to 0.1875
- narrow_affine: bfloat16 [256, 2], P('dp')
- spatial_filter: bfloat16 [2304, 256], P('dp'), may hold values from -0.125 to 0.125
- spatial_affine: bfloat16 [256, 2], P('dp')
- widen_filter: bfloat16 [256, 1024], P('dp'), may hold values from -0.375 to 0.375
- widen_affine: bfloat16 [1024, 2], P('dp')
- shrink_filter: bfloat16 [1024, 512], P('dp'), may hold values from -0.1875 to 0.1875
- shrink_affine: bfloat16 [512, 2], P('dp')
- stride_filter: bfloat16 [4608, 512], P('dp'), may hold values from -0.09375 to 0.09375
- stride_affine: bfloat16 [512, 2], P('dp')
- expand_filter: bfloat16 [512, 2048], P('dp'), may hold values from -0.25 to 0.25
- expand_affine: bfloat16 [2048, 2], P('dp')
- bypass_filter: bfloat16 [1024, 2048], P('dp'), may hold values from -0.1875 to 0.1875
- bypass_affine: bfloat16 [2048, 2], P('dp')
Outputs:
- output_big: bfloat16 [64, 7, 7, 2048], P(('dp', 'outer'))
- output_small: bfloat16 [64, 5, 5, 2048], P(('dp', 'outer'))
- dinput_big: bfloat16 [64, 14, 14, 1024], P(('dp', 'outer'))
- dinput_small: bfloat16 [64, 10, 10, 1024], P(('dp', 'outer'))
- narrow_dfilter: float32 [1024, 256], P('dp')
- narrow_daffine: float32 [256, 2], P('dp')
- spatial_dfilter: float32 [2304, 256], P('dp')
- spatial_daffine: float32 [256, 2], P('dp')
- widen_dfilter: float32 [256, 1024], P('dp')
- widen_daffine: float32 [1024, 2], P('dp')
- shrink_dfilter: float32 [1024, 512], P('dp')
- shrink_daffine: float32 [512, 2], P('dp')
- stride_dfilter: float32 [4608, 512], P('dp')
- stride_daffine: float32 [512, 2], P('dp')
- expand_dfilter: float32 [512, 2048], P('dp')
- expand_daffine: float32 [2048, 2], P('dp')
- bypass_dfilter: float32 [1024, 2048], P('dp')
- bypass_daffine: float32 [2048, 2], P('dp')
Inputs may be any that keep to these rules, and one draw needn't show every extreme that they name: `views_big`: each image's view; each group holds at least one image of each view. `views_small`: each image's view; each group holds at least one image of each view.
All inputs are finite; a program needn't handle non-finite values.
Results may differ from a plain program's by a relative error of at most 0.02.
Values may be sent and summed in bfloat16 or wider, within the bound.
A program may use at most 192 MiB of HBM per device.

v0:
```python
import functools
import types

import jax
import jax.numpy as jnp
from jax import lax
from jax.experimental import pallas as pl
from jax.experimental.pallas import tpu as pltpu
from jax.sharding import PartitionSpec as P

MESH = pl.DeviceIdType.MESH
F32 = jnp.float32
BF16 = jnp.bfloat16


class Place:
    def __init__(self, spare):
        self.spare = spare
        dp = lax.axis_index("dp")
        self.core = lax.axis_index("outer")
        self.rest = lax.rem(dp, spare)
        group = lax.div(dp, spare)
        self.far = lax.div(group, 4)
        self.near = lax.rem(group, 4)
        high, low = lax.div(self.near, 2), lax.rem(self.near, 2)
        self.first = 2 * lax.rem(high + 1 - self.core, 2) + lax.rem(low + self.core, 2)
        self.second = 2 * lax.rem(high + self.core, 2) + lax.rem(low + 1 - self.core, 2)
        self.both = 3 - self.near

    def device(self, far=None, near=None, core=None, rest=None):
        far = self.far if far is None else far
        near = self.near if near is None else near
        core = self.core if core is None else core
        rest = self.rest if rest is None else rest
        return ((far * 4 + near) * self.spare + rest, core)

    def fars(self):
        return [self.device(far=lax.rem(self.far + k, 4)) for k in range(1, 4)]

    def nears(self):
        return [self.device(near=lax.rem(self.near + k, 4)) for k in range(1, 4)]

    def cross_nears(self):
        return [
            self.device(near=lax.rem(self.near + k, 4), core=1 - self.core) for k in range(1, 4)
        ]

    def sibling(self):
        return self.device(core=1 - self.core)

    def rests(self):
        return [
            self.device(rest=lax.rem(self.rest + k, self.spare)) for k in range(1, self.spare)
        ]


def greet(devices):
    barrier = pltpu.get_barrier_semaphore()
    for device in devices:
        pl.semaphore_signal(barrier, inc=1, device_id=device, device_id_type=MESH)
    pl.semaphore_wait(barrier, len(devices))


def send(src, dst, send_sem, recv_sem, device):
    pltpu.make_async_remote_copy(
        src_ref=src,
        dst_ref=dst,
        send_sem=send_sem,
        recv_sem=recv_sem,
        device_id=device,
        device_id_type=MESH,
    ).start()


def await_bytes(like, sem):
    pltpu.make_async_copy(like, like, sem).wait()


class Reduce:
    def __init__(self, place, split, refs):
        self.place = place
        self.split = split
        self.refs = refs

    @staticmethod
    def scratch(rows, width, spare, split):
        piece = width // 2 if split else width
        shapes = []
        for count in Reduce.counts(spare, split):
            shapes.append(pltpu.VMEM((count, rows, piece), F32))
            shapes.append(pltpu.VMEM((rows, piece), F32))
        phases = len(Reduce.counts(spare, split))
        shapes.append(pltpu.SemaphoreType.DMA((phases + 1,)))
        shapes.append(pltpu.SemaphoreType.DMA((phases + 1,)))
        return shapes

    @staticmethod
    def counts(spare, split):
        counts = [1, 3, 3] if split else [7, 3]
        return counts + ([spare - 1] if spare > 1 else [])

    def run(self, src, out, between=None):
        place, split = self.place, self.split
        send_sem, recv_sem = self.refs[-2:]
        width = src.shape[1]
        piece = width // 2
        if split:
            phases = [[place.sibling()], place.nears(), place.fars()]
            mine = pl.ds(pl.multiple_of(place.core * piece, 128), piece)
            other = pl.ds(pl.multiple_of((1 - place.core) * piece, 128), piece)
        else:
            phases = [[place.sibling()] + place.nears() + place.cross_nears(), place.fars()]
        if place.spare > 1:
            phases.append(place.rests())
        held = src
        for p, devices in enumerate(phases):
            slots, total = self.refs[2 * p], self.refs[2 * p + 1]
            crossing = split and p == 0
            sent = src.at[:, other] if crossing else held
            for k, device in enumerate(devices):
                send(sent, slots.at[k], send_sem.at[p], recv_sem.at[p], device)
            if between is not None:
                between(p)
            await_bytes(slots, recv_sem.at[p])
            value = src[:, mine] if crossing else held[...]
            for k in range(len(devices)):
                value = value + slots[k]
            last = p == len(phases) - 1 and not split
            if last:
                out[...] = value
            else:
                total[...] = value
            held = total
        if split:
            send(held, out.at[:, mine], send_sem.at[len(phases)], recv_sem.at[len(phases)], place.sibling())
            out[:, mine] = held[...]
            await_bytes(out.at[:, other], recv_sem.at[len(phases)])
        for p in range(len(phases)):
            await_bytes(self.refs[2 * p], send_sem.at[p])
        if split:
            await_bytes(held, send_sem.at[len(phases)])


class Piece:
    def __init__(self, layer, band=0, bands=1, strip=0, strips=1, halved=True, direct=False):
        self.layer, self.halved, self.direct = layer, halved, direct
        self.band, self.bands, self.strip, self.strips = band, bands, strip, strips

    def sizes(self, shape):
        return shape[-2] // self.bands, shape[-1] // (2 if self.halved else 1) // self.strips

    def window(self, place, shape):
        count, width = self.sizes(shape)
        rows = pl.ds(self.band * count, count)
        if not self.halved:
            return rows, pl.ds(0, width), None
        half, skip = shape[-1] // 2, self.strip * width
        cols = pl.ds(pl.multiple_of(place.core * half + skip, 128), width)
        others = pl.ds(pl.multiple_of((1 - place.core) * half + skip, 128), width)
        return rows, cols, others


class Gather:
    PHASES = 5

    def __init__(self, place, whole, piece, send_sem, recv_sem):
        self.place, self.whole, self.piece = place, whole, piece
        self.halved, self.direct = piece.halved, piece.direct
        self.send_sem, self.recv_sem = send_sem, recv_sem
        self.rows, self.cols, self.others = piece.window(place, whole.shape)

    def part(self, far, near):
        return self.whole.at[far, near, self.rows, self.cols]

    def start(self):
        place = self.place
        for device in place.fars():
            block = self.part(place.far, place.near)
            send(block, block, self.send_sem.at[0], self.recv_sem.at[0], device)

    def near(self):
        place = self.place
        await_bytes(self.part(pl.ds(0, 3), 0), self.recv_sem.at[0])
        block = self.part(pl.ds(0, 4), place.near)
        partners = [place.first, place.second] + ([place.both] if self.direct else [])
        for phase, partner in enumerate(partners, 1):
            send(
                block,
                block,
                self.send_sem.at[phase],
                self.recv_sem.at[phase],
                place.device(near=partner),
            )

    def forward(self):
        place = self.place
        block = self.part(pl.ds(0, 4), place.first)
        await_bytes(block, self.recv_sem.at[1])
        if self.direct:
            return
        send(
            block, block, self.send_sem.at[3], self.recv_sem.at[3], place.device(near=place.second)
        )

    def cross(self):
        place = self.place
        await_bytes(self.part(pl.ds(0, 4), place.second), self.recv_sem.at[2])
        await_bytes(self.part(pl.ds(0, 4), place.both), self.recv_sem.at[3])
        if self.halved:
            block = self.part(pl.ds(0, 4), pl.ds(0, 4))
            send(block, block, self.send_sem.at[4], self.recv_sem.at[4], place.sibling())

    def finish(self):
        if self.halved:
            await_bytes(
                self.whole.at[pl.ds(0, 4), pl.ds(0, 4), self.rows, self.others], self.recv_sem.at[4]
            )

    def settle(self):
        await_bytes(self.part(pl.ds(0, 3), 0), self.send_sem.at[0])
        for phase in (1, 2, 3):
            await_bytes(self.part(pl.ds(0, 4), 0), self.send_sem.at[phase])
        if self.halved:
            await_bytes(self.part(pl.ds(0, 4), pl.ds(0, 4)), self.send_sem.at[4])


class Scatter:
    PHASES = 5

    def __init__(self, place, whole, piece, landing, done, send_sem, recv_sem):
        self.place, self.whole, self.landing, self.done = place, whole, landing, done
        self.direct = piece.direct
        self.send_sem, self.recv_sem = send_sem, recv_sem
        self.rows, self.cols, self.others = piece.window(place, whole.shape)
        self.half = piece.sizes(whole.shape)[1]
        self.base = place.core * (whole.shape[3] // 2) + piece.strip * self.half

    @staticmethod
    def scratch(rows, half):
        return [
            pltpu.VMEM((4, 4, rows, half), BF16),
            pltpu.VMEM((2, 4, rows, half), BF16),
            pltpu.VMEM((4, rows, half), BF16),
            pltpu.VMEM((3, rows, half), BF16),
        ]

    def add(self, near, block):
        blocks = self.half // 128
        whole, base, rows = self.whole, self.base, self.rows

        @pl.loop(0, 4 * blocks)
        def _(i):
            far, b = lax.div(i, blocks), lax.rem(i, blocks)
            here = pl.ds(pl.multiple_of(base + b * 128, 128), 128)
            there = pl.ds(pl.multiple_of(b * 128, 128), 128)
            total = whole[far, near, rows, here].astype(F32) + block[far, :, there].astype(F32)
            whole[far, near, rows, here] = total.astype(BF16)

    def start(self):
        send(
            self.whole.at[pl.ds(0, 4), pl.ds(0, 4), self.rows, self.others],
            self.landing[0],
            self.send_sem.at[0],
            self.recv_sem.at[0],
            self.place.sibling(),
        )

    def second(self):
        place = self.place
        await_bytes(self.landing[0], self.recv_sem.at[0])
        blocks = self.half // 128
        whole, base, rows, block = self.whole, self.base, self.rows, self.landing[0]

        @pl.loop(0, 16 * blocks)
        def _(i):
            group, b = lax.div(i, blocks), lax.rem(i, blocks)
            far, near = lax.div(group, 4), lax.rem(group, 4)
            here = pl.ds(pl.multiple_of(base + b * 128, 128), 128)
            there = pl.ds(pl.multiple_of(b * 128, 128), 128)
            total = whole[far, near, rows, here].astype(F32) + block[far, near, :, there].astype(F32)
            whole[far, near, rows, here] = total.astype(BF16)

        if self.direct:
            landings = (self.landing[1].at[0], self.landing[1].at[1], self.landing[2])
            for k, near in enumerate((place.second, place.both, place.first)):
                send(
                    whole.at[pl.ds(0, 4), near, self.rows, self.cols],
                    landings[k],
                    self.send_sem.at[max(k, 1)],
                    self.recv_sem.at[max(k, 1)],
                    place.device(near=near),
                )
            return
        for k, near in enumerate((place.second, place.both)):
            send(
                whole.at[pl.ds(0, 4), near, self.rows, self.cols],
                self.landing[1].at[k],
                self.send_sem.at[1],
                self.recv_sem.at[1],
                place.device(near=place.second),
            )

    def first(self):
        place = self.place
        await_bytes(self.landing[1], self.recv_sem.at[1])
        if self.direct:
            self.add(place.near, self.landing[1].at[1])
            self.add(place.near, self.landing[1].at[0])
            return
        self.add(place.first, self.landing[1].at[1])
        send(
            self.whole.at[pl.ds(0, 4), place.first, self.rows, self.cols],
            self.landing[2],
            self.send_sem.at[2],
            self.recv_sem.at[2],
            place.device(near=place.first),
        )
        self.add(place.near, self.landing[1].at[0])

    def fars(self):
        place = self.place
        await_bytes(self.landing[2], self.recv_sem.at[2])
        self.add(place.near, self.landing[2])
        for k in range(1, 4):
            far = lax.rem(place.far + k, 4)
            send(
                self.whole.at[far, place.near, self.rows, self.cols],
                self.landing[3].at[k - 1],
                self.send_sem.at[3],
                self.recv_sem.at[3],
                place.device(far=far),
            )

    def cross(self):
        place = self.place
        await_bytes(self.landing[3], self.recv_sem.at[3])
        blocks = self.half // 128
        whole, base, rows, block, done = self.whole, self.base, self.rows, self.landing[3], self.done

        @pl.loop(0, blocks)
        def _(b):
            here = pl.ds(pl.multiple_of(base + b * 128, 128), 128)
            there = pl.ds(pl.multiple_of(b * 128, 128), 128)
            total = whole[place.far, place.near, rows, here].astype(F32)
            for k in range(3):
                total = total + block[k, :, there].astype(F32)
            done[rows, here] = total.astype(BF16)

        half = done.at[self.rows, self.cols]
        send(half, half, self.send_sem.at[4], self.recv_sem.at[4], place.sibling())

    def finish(self):
        await_bytes(self.done.at[self.rows, self.others], self.recv_sem.at[4])

    def settle(self):
        await_bytes(self.landing[0], self.send_sem.at[0])
        await_bytes(self.landing[1], self.send_sem.at[1])
        await_bytes(self.landing[2], self.send_sem.at[2])
        await_bytes(self.landing[3], self.send_sem.at[3])
        await_bytes(self.done.at[self.rows, self.cols], self.send_sem.at[4])
EPS = 1e-05
KERNEL_ID = 1
NARROW, SPATIAL, WIDEN, SHRINK, STRIDE, EXPAND, BYPASS = range(7)
TABLE = 7
LAST = 5
NN = (((1,), (0,)), ((), ()))
NT = (((1,), (1,)), ((), ()))
TN = (((0,), (0,)), ((), ()))


def mul(a, b, dims):
    return lax.dot_general(a, b, dims, preferred_element_type=F32)


def lanes(i, width=128):
    return pl.ds(pl.multiple_of(i * width, width), width)


def normal_parts(value):
    bell = jnp.exp(-0.5 * value * value) * 0.3989422804014327
    step = 1.0 / (1.0 + 0.2316419 * jnp.abs(value))
    series = 1.330274429 * step - 1.821255978
    series = series * step + 1.781477937
    series = series * step - 0.356563782
    series = series * step + 0.319381530
    tail = bell * (series * step)
    cdf = jnp.where(value >= 0.0, 1.0 - tail, tail)
    return cdf, value * bell


class Image:
    def __init__(self, index, group, side, at, half_at):
        self.index, self.group, self.side = index, group, side
        self.half_side = (side - 1) // 2 + 1
        self.at, self.count = at, (side + 1) * 16
        self.half_at, self.half_count = half_at, -(-(self.half_side + 1) * 8 // 16) * 16

    def rows(self, half):
        return pl.ds(self.half_at, self.half_count) if half else pl.ds(self.at, self.count)

    def inside(self, half):
        count = self.half_count if half else self.count
        side = self.half_side if half else self.side
        bits = 3 if half else 4
        place = lax.broadcasted_iota(jnp.int32, (count, 128), 0)
        return jnp.logical_and(
            lax.shift_right_logical(place, bits) < side, lax.bitwise_and(place, (1 << bits) - 1) < side
        )


def images_of(counts, sides):
    images, at, half_at = [], 0, 0
    for group in range(2):
        for _ in range(counts[group]):
            image = Image(len(images), group, sides[group], at, half_at)
            images.append(image)
            at += image.count
            half_at += image.half_count
    return images, at, half_at


def widths_of(c_in, mid1, mid2, c_out):
    return [mid1, mid1, c_in, mid2, mid2, c_out, c_out]


class Layer:
    def __init__(self, width, half, at):
        self.width, self.half, self.at = width, half, at


def rows_piece(whole, start, count, cols):
    rows, pieces = whole.shape[2], []
    while count:
        shard, skip = divmod(start, rows)
        taken = min(rows - skip, count)
        pieces.append(whole[shard // 4, shard % 4, skip : skip + taken, cols])
        start, count = start + taken, count - taken
    return pieces[0] if len(pieces) == 1 else jnp.concatenate(pieces, axis=0)


def store_piece(whole, start, value):
    rows, done = whole.shape[2], 0
    while done < value.shape[0]:
        shard, skip = divmod(start + done, rows)
        taken = min(rows - skip, value.shape[0] - done)
        whole[shard // 4, shard % 4, skip : skip + taken, :] = value[done : done + taken]
        done += taken


def table_places(shares):
    places, at = [], 0
    for share in shares:
        if at % 128 + share > 128:
            at = -(-at // 128) * 128
        places.append(at)
        at += share
    return places


def step_kernel(spare, images, widths, refs):
    place = Place(spare)
    full_rows, half_rows = refs.x.shape[0], refs.cot.shape[0]
    hot, cnt = refs.hot_v, refs.cnt
    whole = refs.whole
    c_in, mid1, mid2, c_out = widths
    loads = []

    def load(src, dst):
        copy = pltpu.make_async_copy(src, dst, refs.load_sem.at[len(loads)])
        copy.start()
        loads.append(copy)
        return copy

    gathers = [
        Gather(place, whole[piece.layer], piece, refs.gather_send.at[k], refs.gather_recv.at[k])
        for k, piece in enumerate(PIECES)
    ]
    shard_loads = [
        load(
            refs.shards[item.piece.layer].at[item.rows, item.cols], item.part(place.far, place.near)
        )
        for item in gathers
    ]
    load_hot = load(refs.hot, hot)
    load_x = load(refs.x, refs.x_v)
    load_cot = load(refs.cot, refs.cot_v)
    scatters = [
        Scatter(
            place,
            whole[piece.layer],
            piece,
            refs.landing[k],
            refs.done[piece.layer],
            refs.scatter_send.at[k],
            refs.scatter_recv.at[k],
        )
        for k, piece in enumerate(PIECES[:-1])
    ]

    def pieces_of(items, layer):
        return [item for item, piece in zip(items, PIECES) if piece.layer == layer]

    def arrive(layer):
        for item in pieces_of(gathers, layer):
            item.finish()

    def let_go(layer):
        for item in pieces_of(gathers, layer):
            item.settle()

    def send_off(layer):
        for item in pieces_of(scatters, layer):
            item.start()

    def begin(k):
        shard_loads[k].wait()
        gathers[k].start()

    points = []

    def point():
        now = len(points)
        points.append(now)
        for step, *items in PLAN.get(now, ()):
            for k in items:
                if step is BEGIN:
                    begin(k)
                else:
                    step(gathers[k] if step in GATHER_STEPS else scatters[k])

    greet([place.sibling()] + place.nears() + place.cross_nears() + place.fars() + place.rests())

    layers, lane = [], 0
    for k, width in enumerate(widths_of(*widths)):
        layers.append(Layer(width, k in (STRIDE, EXPAND, BYPASS), lane))
        lane += width
        layers[k].normed, layers[k].slope = refs.normed[k], refs.slope[k]
        layers[k].affine, layers[k].scale = refs.affine[k], refs.scale[k]

    def reduce(way, k, during=None):
        def between(p):
            if p < 2:
                point()
                if during is not None:
                    during(p)

        slots = refs.slots[way if k in (NARROW, LAST) else 0][k]
        Reduce(place, k == LAST, list(slots) + list(refs.sums_sem[way][k])).run(
            refs.given[way][k], refs.total[way][k], between
        )
        point()

    def hot_row(image, view):
        row = 2 * image.index + view
        return hot[row : row + 1, :]

    def of_image(image, by_view):
        row = 2 * image.group
        return hot_row(image, 0) * by_view[row : row + 1] + hot_row(image, 1) * by_view[row + 1 : row + 2]

    def by_view(values):
        out = []
        for group in range(2):
            for view in range(2):
                total = None
                for image in images:
                    if image.group == group:
                        term = values[image.index] * hot_row(image, view)
                        total = term if total is None else total + term
                out.append(total)
        return out

    def put_sums(st, cols, firsts, seconds):
        st[:, cols] = jnp.concatenate(by_view(firsts) + by_view(seconds), axis=0)

    def column_sum(value):
        return jnp.sum(value, axis=0, keepdims=True)

    def field_sums(layer, st, field, i, masked, cols=None):
        firsts, seconds = [], []
        for image in images:
            z = field(image, i)
            if masked:
                z = jnp.where(image.inside(layer.half), z, 0.0)
            firsts.append(column_sum(z))
            seconds.append(column_sum(z * z))
        put_sums(st, lanes(i) if cols is None else cols, firsts, seconds)

    def statistics(total):
        counted = cnt[0:4, :]
        mean = total[0:4] / counted
        return mean, lax.rsqrt(total[4:8] / counted - mean * mean + EPS)

    def normed_of(layer, image, cols, z, mean, scale):
        stretch = of_image(image, scale)
        layer.scale[image.index : image.index + 1, cols] = stretch
        return (z - of_image(image, mean)) * stretch

    def forward(name, field, sink, extra=None):
        layer = layers[name]

        @pl.loop(0, layer.width // 128)
        def _(i):
            cols = lanes(i)
            mean, scale = statistics(refs.total[0][name][:, cols])
            gain, bias = layer.affine[0:1, cols], layer.affine[1:2, cols]
            for image in images:
                rows, inside = image.rows(layer.half), image.inside(layer.half)
                normed = normed_of(layer, image, cols, field(image, i), mean, scale)
                value = normed * gain + bias
                if extra is not None:
                    value = value + extra[rows, cols].astype(F32)
                cdf, rest = normal_parts(value)
                layer.normed[rows, cols] = normed.astype(BF16)
                layer.slope[rows, cols] = jnp.where(inside, cdf + rest, 0.0).astype(BF16)
                sink(image, i, jnp.where(inside, value * cdf, 0.0))

    def gradient_sums(name, grad, st):
        layer = layers[name]

        @pl.loop(0, layer.width // 128)
        def _(i):
            cols = lanes(i)
            firsts, seconds = [], []
            for image in images:
                g = grad(image, i)
                firsts.append(column_sum(g))
                seconds.append(column_sum(g * layer.normed[image.rows(layer.half), cols].astype(F32)))
            put_sums(st, cols, firsts, seconds)

    def gradient(name, grad, sums, sink=None):
        layer = layers[name]

        @pl.loop(0, layer.width // 128)
        def _(i):
            cols = lanes(i)
            first, second = sums(i)
            here = pl.ds(pl.multiple_of(layer.at + i * 128, 128), 128)
            refs.daffine_v[0:1, here] = column_sum(second)
            refs.daffine_v[1:2, here] = column_sum(first)
            first, second = first / cnt[0:4, :], second / cnt[0:4, :]
            gain = layer.affine[0:1, cols]
            for image in images:
                rows = image.rows(layer.half)
                stretch = gain * layer.scale[image.index : image.index + 1, cols]
                normed = layer.normed[rows, cols].astype(F32)
                value = stretch * (grad(image, i) - of_image(image, first) - normed * of_image(image, second))
                value = jnp.where(image.inside(layer.half), value, 0.0)
                if sink is None:
                    layer.normed[rows, cols] = value.astype(BF16)
                else:
                    sink(image, i, value)

    def totals_of(name):
        def sums(i):
            total = refs.total[1][name][:, lanes(i)]
            return total[0:4], total[4:8]

        return sums

    def shifted(target, image, i, value):
        width = target.shape[1] // 3
        rows = pl.ds(16 + image.at, image.count)
        for q in range(3):
            moved = value if q == 1 else pltpu.roll(value, 1 if q == 0 else image.count - 1, 0)
            target[rows, pl.ds(pl.multiple_of(q * width + i * 128, 128), 128)] = moved.astype(BF16)

    def clear_ends(target, top, from_row):
        target[0:top, :] = jnp.zeros((top, target.shape[1]), target.dtype)
        target[from_row:, :] = jnp.zeros((target.shape[0] - from_row, target.shape[1]), target.dtype)

    def strided(start):
        return pl.ds(start, 8, stride=2)

    F, G, K, S = refs.F, refs.G, refs.K, refs.S
    x_v, taps1, act_spatial, upper = refs.x_v, refs.taps1, refs.act_spatial, refs.upper
    taps2, act_stride, even, grad3 = refs.taps2, refs.act_stride, refs.even, refs.grad3
    clear_ends(taps1, 16, 16 + full_rows)
    clear_ends(grad3, 16, 16 + full_rows)
    blocks2 = mid2 // 128
    K[:, 0:32, :] = jnp.zeros((blocks2, 32, 128), F32)
    K[:, 32 + full_rows :, :] = jnp.zeros((blocks2, K.shape[1] - 32 - full_rows, 128), F32)
    EVEN, SPREAD = refs.EVEN, refs.SPREAD
    SPREAD[...] = jnp.zeros(SPREAD.shape, F32)

    places = table_places([layer.width // 16 for layer in layers])

    def spread_affine(k):
        table, layer = whole[TABLE], layers[k]
        share = layer.width // 16
        row, skip = divmod(places[k], 128)
        to = lax.broadcasted_iota(jnp.int32, (16, 128), 1)
        owner = lax.broadcasted_iota(jnp.int32, (16, 128), 0)
        pick_from = lax.broadcasted_iota(jnp.int32, (128, 128), 0)
        pick_to = lax.broadcasted_iota(jnp.int32, (128, 128), 1)
        chosen = (pick_from == skip + lax.rem(pick_to, share)).astype(BF16)
        for kind in range(2):
            held = [
                table[g // 4, g % 4, :, :].astype(F32)[row + 4 * kind : row + 4 * kind + 1] for g in range(16)
            ]
            spread = mul(jnp.concatenate(held, axis=0).astype(BF16), chosen, NN)
            for b in range(layer.width // 128):
                mine = jnp.where(lax.div(b * 128 + to, share) == owner, spread, 0.0)
                layer.affine[kind : kind + 1, b * 128 : (b + 1) * 128] = column_sum(mine)

    load_hot.wait()
    load_x.wait()
    point()

    def plain(buffer):
        return lambda image, i: buffer[image.rows(False), lanes(i)]

    def plain_half(buffer):
        return lambda image, i: buffer[image.rows(True), lanes(i)]

    def halves(buffer, base):
        blocks = F.shape[1] // 128

        def field(image, i):
            band = base + lax.div(i, blocks)
            rows = pl.ds(pl.multiple_of(band * half_rows + image.half_at, 8), image.half_count)
            return buffer[rows, lanes(lax.rem(i, blocks))]

        return field

    arrive(NARROW)
    F[0:full_rows, 0:mid1] = mul(x_v[...], whole[NARROW][...].reshape(c_in, mid1), NN)

    @pl.loop(0, mid1 // 128)
    def _(i):
        field_sums(layers[NARROW], refs.given[0][NARROW], plain(F), i, False)

    pixels = []
    for image in images:
        pixels.append(jnp.full((1, 128), float(image.side * image.side), F32))
    empty = [jnp.zeros((1, 128), F32) for _ in images]
    put_sums(refs.given[0][NARROW], pl.ds(mid1, 128), pixels, empty)

    def during(p):
        if p == 0:
            for k in (NARROW, SPATIAL, WIDEN):
                spread_affine(k)

    point()
    reduce(0, NARROW, during)
    cnt[...] = refs.total[0][NARROW][:, mid1 : mid1 + 128]
    forward(NARROW, plain(F), functools.partial(shifted, taps1))

    point()
    arrive(SPATIAL)
    for r in range(3):
        kernel = rows_piece(whole[SPATIAL], r * 3 * mid1, 3 * mid1, slice(None))
        term = mul(taps1[16 * r : 16 * r + full_rows, :], kernel, NN)
        F[0:full_rows, 0:mid1] = term if r == 0 else F[0:full_rows, 0:mid1] + term

    @pl.loop(0, mid1 // 128)
    def _(i):
        field_sums(layers[SPATIAL], refs.given[0][SPATIAL], plain(F), i, True)

    def during(p):
        if p == 0:
            for k in (SHRINK, STRIDE):
                spread_affine(k)

    point()
    reduce(0, SPATIAL, during)

    def to_spatial(image, i, value):
        act_spatial[image.rows(False), lanes(i)] = value.astype(BF16)

    forward(SPATIAL, plain(F), to_spatial)

    point()
    arrive(WIDEN)

    @pl.loop(0, c_in // 256)
    def _(j):
        cols = lanes(j, 256)
        F[0:full_rows, cols] = mul(act_spatial[...], whole[WIDEN][:, :, :, cols].reshape(mid1, 256), NN)
        for k in range(2):
            field_sums(layers[WIDEN], refs.given[0][WIDEN], plain(F), 2 * j + k, False)

    def during(p):
        if p == 0:
            for k in (EXPAND, BYPASS):
                spread_affine(k)

    point()
    reduce(0, WIDEN, during)

    def to_upper(image, i, value):
        upper[image.rows(False), lanes(i)] = value.astype(BF16)
        rows = image.rows(False)
        EVEN[rows, :] = value
        for pair in range(image.half_count // 16):
            both = [EVEN[strided(image.at + 32 * min(2 * pair + k, image.half_side - 1)), :] for k in range(2)]
            here = pl.ds(image.half_at + 16 * pair, 16)
            even[here, lanes(i)] = jnp.concatenate(both, axis=0).astype(BF16)

    forward(WIDEN, plain(F), to_upper, x_v)

    point()
    arrive(SHRINK)

    @pl.loop(0, mid2 // 256)
    def _(j):
        cols = lanes(j, 256)
        F[0:full_rows, cols] = mul(upper[...], whole[SHRINK][:, :, :, cols].reshape(c_in, 256), NN)
        for k in range(2):
            field_sums(layers[SHRINK], refs.given[0][SHRINK], plain(F), 2 * j + k, False)

    point()
    reduce(0, SHRINK)

    def to_shrink(image, i, value):
        K[i, pl.ds(32 + image.at, image.count), :] = value

    forward(SHRINK, plain(F), to_shrink)

    for image in images:

        @pl.loop(0, image.half_count // 16)
        def _(pair):
            rows = pl.ds(pl.multiple_of(image.half_at + 16 * pair, 16), 16)
            for r in range(3):
                for q in range(3):
                    start = 32 + image.at + 64 * pair + (r - 1) * 16 + q - 1
                    for b in range(blocks2):
                        both = [K[b, strided(start + 32 * k), :] for k in range(2)]
                        at = (3 * r + q) * mid2 + b * 128
                        taps2[rows, at : at + 128] = jnp.concatenate(both, axis=0).astype(BF16)

    point()
    arrive(STRIDE)

    @pl.loop(0, mid2 // 256)
    def _(j):
        cols = lanes(j, 256)
        depth = 9 * mid2 // 4
        for far in range(4):
            kernel = whole[STRIDE][far, :, :, cols].reshape(depth, 256)
            term = mul(taps2[:, far * depth : (far + 1) * depth], kernel, NN)
            G[:, cols] = term if far == 0 else G[:, cols] + term
        for k in range(2):
            field_sums(layers[STRIDE], refs.given[0][STRIDE], plain_half(G), 2 * j + k, True)

    def bypass_field():
        arrive(BYPASS)

        @pl.loop(0, c_out // 256)
        def _(j):
            value = mul(even[...], whole[BYPASS][:, :, :, lanes(j, 256)].reshape(c_in, 256), NN)
            blocks = c_in // 256
            rows = pl.ds(pl.multiple_of((2 + lax.div(j, blocks)) * half_rows, 8), half_rows)
            F[rows, lanes(lax.rem(j, blocks), 256)] = value
            for k in range(2):
                i = 2 * j + k
                cols = pl.ds(pl.multiple_of(c_out + i * 128, 128), 128)
                field_sums(layers[BYPASS], refs.given[0][LAST], halves(F, 2), i, True, cols)

    point()
    reduce(0, STRIDE)

    def to_stride(image, i, value):
        act_stride[image.rows(True), lanes(i)] = value.astype(BF16)

    forward(STRIDE, plain_half(G), to_stride)

    point()
    arrive(EXPAND)

    @pl.loop(0, c_out // 256)
    def _(j):
        value = mul(act_stride[...], whole[EXPAND][:, :, :, lanes(j, 256)].reshape(mid2, 256), NN)
        blocks = c_in // 256
        rows = pl.ds(pl.multiple_of(lax.div(j, blocks) * half_rows, 8), half_rows)
        F[rows, lanes(lax.rem(j, blocks), 256)] = value
        for k in range(2):
            field_sums(layers[EXPAND], refs.given[0][LAST], halves(F, 0), 2 * j + k, True)

    point()
    bypass_field()
    reduce(0, LAST)
    load_cot.wait()
    expand_z, bypass_z = halves(F, 0), halves(F, 2)

    @pl.loop(0, c_out // 128)
    def _(i):
        cols = lanes(i)
        upper_cols = pl.ds(pl.multiple_of(c_out + i * 128, 128), 128)
        stats_e = statistics(refs.total[0][LAST][:, cols])
        stats_b = statistics(refs.total[0][LAST][:, upper_cols])
        el, bl = layers[EXPAND], layers[BYPASS]
        firsts, seconds, thirds = [], [], []
        for image in images:
            rows, inside = image.rows(True), image.inside(True)
            normed_e = normed_of(el, image, cols, expand_z(image, i), *stats_e)
            normed_b = normed_of(bl, image, cols, bypass_z(image, i), *stats_b)
            value = normed_e * el.affine[0:1, cols] + el.affine[1:2, cols]
            value = value + (normed_b * bl.affine[0:1, cols] + bl.affine[1:2, cols])
            cdf, rest = normal_parts(value)
            el.normed[rows, cols] = normed_e.astype(BF16)
            bl.normed[rows, cols] = normed_b.astype(BF16)
            grad = jnp.where(inside, refs.cot_v[rows, cols].astype(F32) * (cdf + rest), 0.0)
            refs.cot_v[rows, cols] = (value * cdf).astype(BF16)
            blocks = F.shape[1] // 128
            band = lax.div(i, blocks)
            here = pl.ds(pl.multiple_of(band * half_rows + image.half_at, 8), image.half_count)
            F[here, lanes(lax.rem(i, blocks))] = grad
            firsts.append(column_sum(grad))
            seconds.append(column_sum(grad * normed_e))
            thirds.append(column_sum(grad * normed_b))
        put_sums(refs.given[1][LAST], cols, firsts, seconds)
        put_sums(refs.given[1][LAST], upper_cols, thirds, thirds)

    store_out = pltpu.make_async_copy(refs.cot_v, refs.out, refs.store_sem.at[0])
    store_out.start()
    point()
    reduce(1, LAST)

    def sums_expand(i):
        total = refs.total[1][LAST][:, lanes(i)]
        return total[0:4], total[4:8]

    def sums_bypass(i):
        first = refs.total[1][LAST][:, lanes(i)]
        second = refs.total[1][LAST][:, pl.ds(pl.multiple_of(c_out + i * 128, 128), 128)]
        return first[0:4], second[0:4]

    gradient(EXPAND, halves(F, 0), sums_expand)
    gradient(BYPASS, halves(F, 0), sums_bypass)
    expand_grad, bypass_grad = layers[EXPAND].normed, layers[BYPASS].normed

    point()
    @pl.loop(0, mid2 // 256)
    def _(j):
        kernel = whole[EXPAND][pl.ds(2 * j, 2)].reshape(256, c_out)
        cols = lanes(j, 256)
        G[:, cols] = mul(expand_grad[...], kernel, NT) * layers[STRIDE].slope[:, cols].astype(F32)

    gradient_sums(STRIDE, plain_half(G), refs.given[1][STRIDE])

    def filter_grad(name, left, right, fars):
        let_go(name)
        target = whole[name]
        shard, columns = target.shape[2], target.shape[3]
        depth = fars * 4 * shard
        width = min(columns, 512 if depth <= 512 else 256)

        @pl.loop(0, (4 // fars) * (columns // width))
        def _(i):
            j, b = lax.div(i, columns // width), lax.rem(i, columns // width)
            value = mul(left[:, lanes(j, depth)], right[:, lanes(b, width)], TN)
            target[pl.ds(j * fars, fars), :, :, lanes(b, width)] = value.astype(BF16).reshape(fars, 4, shard, width)

    def during(p):
        if p == 0:
            filter_grad(EXPAND, act_stride, expand_grad, 2)
            send_off(EXPAND)
        if p == 1:

            @pl.loop(0, 4)
            def _(j):
                kernel = whole[BYPASS][j].reshape(256, c_out)
                S[pl.ds(pl.multiple_of(j * half_rows, 8), half_rows), :] = mul(bypass_grad[...], kernel, NT)

            filter_grad(BYPASS, even, bypass_grad, 1)
            send_off(BYPASS)

    point()
    reduce(1, STRIDE, during)
    gradient(STRIDE, plain_half(G), totals_of(STRIDE))
    stride_grad = layers[STRIDE].normed

    point()
    K[...] = jnp.zeros(K.shape, F32)
    for r in range(3):
        for q in range(3):
            kernel = rows_piece(whole[STRIDE], (3 * r + q) * mid2, mid2, slice(None))
            F[0:half_rows, 0:mid2] = mul(stride_grad[...], kernel, NT)
            for image in images:

                @pl.loop(0, image.half_side)
                def _(i):
                    there = strided(32 + image.at + 32 * i + (r - 1) * 16 + q - 1)
                    here = pl.ds(pl.multiple_of(image.half_at + 8 * i, 8), 8)
                    for b in range(blocks2):
                        K[b, there, :] = K[b, there, :] + F[here, b * 128 : (b + 1) * 128]

    @pl.loop(0, mid2 // 128)
    def _(i):
        cols = lanes(i)
        firsts, seconds = [], []
        for image in images:
            rows = pl.ds(32 + image.at, image.count)
            g = K[i, rows, :] * layers[SHRINK].slope[image.rows(False), cols].astype(F32)
            K[i, rows, :] = g
            firsts.append(column_sum(g))
            seconds.append(column_sum(g * layers[SHRINK].normed[image.rows(False), cols].astype(F32)))
        put_sums(refs.given[1][SHRINK], cols, firsts, seconds)

    def during(p):
        if p == 0:
            filter_grad(STRIDE, taps2, stride_grad, 1)
            send_off(STRIDE)

    point()
    reduce(1, SHRINK, during)
    gradient(SHRINK, lambda image, i: K[i, pl.ds(32 + image.at, image.count), :], totals_of(SHRINK))
    shrink_grad = layers[SHRINK].normed

    point()

    @pl.loop(0, 4)
    def _(j):
        cols = lanes(j, 256)
        kernel = whole[SHRINK][j].reshape(256, mid2)
        F[0:full_rows, cols] = mul(shrink_grad[...], kernel, NT)

    @pl.loop(0, c_in // 128)
    def _(i):
        cols = lanes(i)
        firsts, seconds = [], []
        for image in images:
            rows = image.rows(False)
            for j in range(image.half_side):
                start = pl.multiple_of(lax.div(i, 2) * half_rows + image.half_at + 8 * j, 8)
                SPREAD[strided(image.at + 32 * j), :] = S[pl.ds(start, 8), lanes(lax.rem(i, 2))]
            g = (F[rows, cols] + SPREAD[rows, :]) * layers[WIDEN].slope[rows, cols].astype(F32)
            F[rows, cols] = g
            firsts.append(column_sum(g))
            seconds.append(column_sum(g * layers[WIDEN].normed[rows, cols].astype(F32)))
        put_sums(refs.given[1][WIDEN], cols, firsts, seconds)

    def during(p):
        if p == 0:
            filter_grad(SHRINK, upper, shrink_grad, 1)
            send_off(SHRINK)

    point()
    reduce(1, WIDEN, during)
    gradient(WIDEN, plain(F), totals_of(WIDEN))
    widen_grad = layers[WIDEN].normed

    point()
    S[0:full_rows, :] = mul(widen_grad[...], whole[WIDEN][...].reshape(mid1, c_in), NT) * layers[SPATIAL].slope[...].astype(F32)
    gradient_sums(SPATIAL, plain(S), refs.given[1][SPATIAL])

    def during(p):
        if p == 0:
            filter_grad(WIDEN, act_spatial, widen_grad, 4)
            send_off(WIDEN)

    point()
    reduce(1, SPATIAL, during)
    gradient(SPATIAL, plain(S), totals_of(SPATIAL), functools.partial(shifted, grad3))

    point()
    for r in range(3):
        kernel = jnp.concatenate(
            [rows_piece(whole[SPATIAL], (3 * r + 2 - q) * mid1, mid1, slice(None)) for q in range(3)], axis=1
        )
        term = mul(grad3[16 * (2 - r) : 16 * (2 - r) + full_rows, :], kernel, NT)
        S[0:full_rows, :] = term if r == 0 else S[0:full_rows, :] + term
    S[0:full_rows, :] = S[0:full_rows, :] * layers[NARROW].slope[...].astype(F32)
    gradient_sums(NARROW, plain(S), refs.given[1][NARROW])

    def during(p):
        if p == 0:
            let_go(SPATIAL)
            for r in range(3):
                value = mul(taps1[16 * r : 16 * r + full_rows, :], grad3[16 : 16 + full_rows, mid1 : 2 * mid1], TN)
                store_piece(whole[SPATIAL], r * 3 * mid1, value.astype(BF16))
            send_off(SPATIAL)

    point()
    reduce(1, NARROW, during)
    gradient(NARROW, plain(S), totals_of(NARROW))
    narrow_grad = layers[NARROW].normed

    point()
    for j in range(4):
        upper[0:256, j * mid1 : (j + 1) * mid1] = whole[NARROW][j].reshape(256, mid1)
    filter_grad(NARROW, x_v, narrow_grad, 1)
    send_off(NARROW)
    point()
    for j in range(4):
        cols = slice(j * 256, (j + 1) * 256)
        kernel = upper[0:256, j * mid1 : (j + 1) * mid1]
        x_v[:, cols] = (F[0:full_rows, cols] + mul(narrow_grad[...], kernel, NT)).astype(BF16)
        point()
    stores = [
        pltpu.make_async_copy(x_v, refs.dinput, refs.store_sem.at[1]),
        pltpu.make_async_copy(refs.daffine_v, refs.daffine, refs.store_sem.at[2]),
    ]
    for store in stores:
        store.start()
    point()
    for k in (EXPAND, BYPASS, STRIDE, SHRINK, WIDEN, SPATIAL, NARROW):
        for item in pieces_of(scatters, k):
            item.finish()
        stores.append(pltpu.make_async_copy(refs.done[k], refs.dfilter[k], refs.store_sem.at[3 + k]))
        stores[-1].start()
    for item in scatters:
        item.settle()
    let_go(TABLE)
    store_out.wait()
    for store in stores:
        store.wait()


PIECES = [
    Piece(NARROW, direct=True),
    Piece(SPATIAL),
    Piece(WIDEN),
    Piece(SHRINK),
    Piece(STRIDE, 0, 2, 0, 2),
    Piece(STRIDE, 0, 2, 1, 2),
    Piece(STRIDE, 1, 2, 0, 2),
    Piece(STRIDE, 1, 2, 1, 2),
    Piece(EXPAND, 0, 1, 0, 2),
    Piece(EXPAND, 0, 1, 1, 2),
    Piece(BYPASS, 0, 1, 0, 4),
    Piece(BYPASS, 0, 1, 1, 4),
    Piece(BYPASS, 0, 1, 2, 4),
    Piece(BYPASS, 0, 1, 3, 4),
    Piece(TABLE, halved=False, direct=True),
]
N, S, W, K, T0, T1, T2, T3, E0, E1, B0, B1, B2, B3, TAB = range(15)
BEGIN = object()
GATHER_STEPS = (Gather.near, Gather.forward, Gather.cross)
NEAR, FORWARD, CROSS = GATHER_STEPS
R2, R3, R4, R5 = Scatter.second, Scatter.first, Scatter.fars, Scatter.cross
PLAN = {
    0: [
        (BEGIN, TAB, N),
        (NEAR, TAB, N),
        (BEGIN, S, W, K, T0),
        (FORWARD, TAB, N),
        (CROSS, N),
        (NEAR, S),
    ],
    1: [(CROSS, TAB)],
    2: [(FORWARD, S), (NEAR, W, K), (BEGIN, T1)],
    3: [(CROSS, S)],
    4: [(FORWARD, W), (NEAR, T0), (BEGIN, T2)],
    6: [(CROSS, W)],
    7: [(FORWARD, K, T0), (NEAR, T1), (BEGIN, T3)],
    8: [(CROSS, K, T0)],
    9: [(NEAR, T2), (BEGIN, E0)],
    12: [(FORWARD, T1, T2), (NEAR, T3), (BEGIN, E1)],
    13: [(CROSS, T1, T2)],
    14: [(NEAR, E0), (FORWARD, T3), (BEGIN, B0)],
    17: [(FORWARD, E0), (NEAR, E1), (BEGIN, B1)],
    18: [(CROSS, T3, E0)],
    19: [(NEAR, B0), (BEGIN, B2)],
    22: [(FORWARD, E1, B0), (NEAR, B1), (BEGIN, B3)],
    23: [(CROSS, E1, B0)],
    24: [(NEAR, B2), (FORWARD, B1)],
    25: [(NEAR, B3), (FORWARD, B2), (CROSS, B1)],
    26: [(FORWARD, B3), (CROSS, B2, B3)],
    37: [(R2, E0, E1)],
    38: [(R2, B0)],
    39: [(R3, E0, E1), (R2, B1)],
    40: [(R4, E0)],
    41: [(R3, B0, B1), (R2, B2), (R4, E1)],
    42: [(R5, E0)],
    43: [(R2, B3), (R3, B2), (R4, B0)],
    44: [(R2, T0), (R4, B1)],
    46: [(R3, B3, T0), (R2, T1), (R4, B2)],
    47: [(R5, E1, B0)],
    48: [(R2, T2), (R4, B3)],
    49: [(R3, T1), (R4, T0)],
    51: [(R3, T2), (R2, T3), (R4, T1)],
    52: [(R5, B1, B2)],
    53: [(R2, K), (R3, T3), (R4, T2)],
    54: [(R2, W)],
    56: [(R3, K, W), (R4, T3)],
    57: [(R5, B3, T0, T1), (R2, S)],
    58: [(R3, S), (R4, K, W)],
    60: [(R4, S), (R5, T2, T3)],
    61: [(R5, K, W)],
    62: [(R2, N)],
    63: [(R5, S)],
    65: [(R3, N), (R4, N), (R5, N)],
}


def spare_groups(spare):
    count = lax.axis_size("dp")
    return [list(range(at, at + spare)) for at in range(0, count, spare)]


def padded(field, rows, across):
    side = field.shape[1]
    field = jnp.pad(field, ((0, 0), (0, rows - side), (0, across - side), (0, 0)))
    return field.reshape(-1, field.shape[3])


def local(
    input_big,
    input_small,
    views_big,
    views_small,
    cotan_big,
    cotan_small,
    *params,
):
    filters, affines = params[0::2], params[1::2]
    devices = lax.axis_size("dp")
    spare = devices // 16
    inputs, cotans, views = (input_big, input_small), (cotan_big, cotan_small), (views_big, views_small)
    counts = [item.shape[0] for item in inputs]
    images, full_rows, half_rows = images_of(counts, [item.shape[1] for item in inputs])
    c_in, c_out = input_big.shape[3], cotan_big.shape[3]
    mid1, mid2 = filters[NARROW].shape[1], filters[SHRINK].shape[1]
    widths = (c_in, mid1, mid2, c_out)
    wide = widths_of(*widths)
    by_group = [next(image for image in images if image.group == g) for g in range(2)]
    x = jnp.concatenate([padded(inputs[g], by_group[g].count // 16, 16) for g in range(2)])
    cot = jnp.concatenate([padded(cotans[g], by_group[g].half_count // 8, 8) for g in range(2)])
    view = jnp.concatenate(views)
    hot = (view[:, None] == jnp.arange(2, dtype=jnp.int32)[None, :]).astype(F32)
    hot = jnp.broadcast_to(hot.reshape(-1, 1), (2 * len(images), 128))

    parts = [item.T for item in affines]
    shards = list(filters)
    if spare > 1:
        groups = spare_groups(spare)
        shards = [lax.all_gather(item, "dp", axis_index_groups=groups, tiled=True) for item in filters]
        gathered = lax.all_gather(jnp.concatenate(parts, axis=1), "dp", axis_index_groups=groups)
        parts, at = [], 0
        for item in affines:
            share = item.shape[0]
            parts.append(jnp.moveaxis(gathered[:, :, at : at + share], 0, 1).reshape(2, -1))
            at += share
    places = table_places([item.shape[1] for item in parts]) + [512]
    parts = [
        jnp.pad(item, ((0, 0), (0, places[k + 1] - places[k] - item.shape[1]))) for k, item in enumerate(parts)
    ]
    shards.append(jnp.pad(jnp.concatenate(parts, axis=1).reshape(8, 128), ((0, 8), (0, 0))))
    shapes = [item.shape for item in shards]
    lane_total = sum(wide)

    def field(*shape):
        return pltpu.VMEM(shape, F32)

    def rounded(*shape):
        return pltpu.VMEM(shape, BF16)

    def layer_rows(k):
        return half_rows if k in (STRIDE, EXPAND, BYPASS) else full_rows

    rounds = [wide[:5] + [2 * c_out], wide[:5] + [2 * c_out]]
    rounds[0][NARROW] += 128
    sums = [[Reduce.scratch(8, width, spare, k == LAST) for k, width in enumerate(way)] for way in rounds]
    slots = [[item[:-2] for item in way] for way in sums]
    slots[1] = [item if k in (NARROW, LAST) else [] for k, item in enumerate(slots[1])]
    operands = dict(x=x, cot=cot, hot=hot, shards=shards)
    results = dict(
        out=jax.ShapeDtypeStruct((half_rows, c_out), BF16),
        dinput=jax.ShapeDtypeStruct((full_rows, c_in), BF16),
        daffine=jax.ShapeDtypeStruct((8, lane_total), F32),
        dfilter=[jax.ShapeDtypeStruct(shape, BF16) for shape in shapes[:7]],
    )
    scratch = dict(
        whole=[rounded(4, 4, *shape) for shape in shapes],
        done=[rounded(*shape) for shape in shapes[:7]],
        landing=[Scatter.scratch(*piece.sizes(shapes[piece.layer])) for piece in PIECES[:-1]],
        normed=[rounded(layer_rows(k), wide[k]) for k in range(7)],
        slope=[None if k in (EXPAND, BYPASS) else rounded(layer_rows(k), wide[k]) for k in range(7)],
        affine=[field(8, width) for width in wide],
        scale=[field(-(-len(images) // 8) * 8, width) for width in wide],
        x_v=rounded(full_rows, c_in),
        cot_v=rounded(half_rows, c_out),
        hot_v=field(*hot.shape),
        cnt=field(8, 128),
        daffine_v=field(8, lane_total),
        F=field(max(full_rows, 4 * half_rows), c_in),
        G=field(half_rows, mid2),
        S=field(max(full_rows, 4 * half_rows), mid1),
        K=field(mid2 // 128, full_rows + 64, 128),
        EVEN=field(full_rows, 128),
        SPREAD=field(full_rows, 128),
        taps1=rounded(full_rows + 32, 3 * mid1),
        grad3=rounded(full_rows + 32, 3 * mid1),
        act_spatial=rounded(full_rows, mid1),
        upper=rounded(full_rows, c_in),
        taps2=rounded(half_rows, 9 * mid2),
        act_stride=rounded(half_rows, mid2),
        even=rounded(half_rows, c_in),
        given=[[field(8, width) for width in way] for way in rounds],
        total=[[field(8, width) for width in way] for way in rounds],
        slots=slots,
        sums_sem=[[item[-2:] for item in way] for way in sums],
        load_sem=pltpu.SemaphoreType.DMA((len(PIECES) + 3,)),
        store_sem=pltpu.SemaphoreType.DMA((16,)),
        gather_send=pltpu.SemaphoreType.DMA((len(PIECES), Gather.PHASES)),
        gather_recv=pltpu.SemaphoreType.DMA((len(PIECES), Gather.PHASES)),
        scatter_send=pltpu.SemaphoreType.DMA((len(PIECES), Scatter.PHASES)),
        scatter_recv=pltpu.SemaphoreType.DMA((len(PIECES), Scatter.PHASES)),
    )
    flat_in, in_tree = jax.tree.flatten(operands)
    flat_out, out_tree = jax.tree.flatten(results)
    flat_scratch, scratch_tree = jax.tree.flatten(scratch)

    def kernel(*flat):
        here = len(flat_in) + len(flat_out)
        refs = jax.tree.unflatten(in_tree, flat[: len(flat_in)])
        refs |= jax.tree.unflatten(out_tree, flat[len(flat_in) : here])
        refs |= jax.tree.unflatten(scratch_tree, flat[here:])
        step_kernel(spare, images, widths, types.SimpleNamespace(**refs))

    flat_out = pl.pallas_call(
        kernel,
        out_shape=flat_out,
        in_specs=[pl.BlockSpec(memory_space=pl.ANY)] * len(flat_in),
        out_specs=[pl.BlockSpec(memory_space=pl.ANY)] * len(flat_out),
        scratch_shapes=flat_scratch,
        compiler_params=pltpu.CompilerParams(
            collective_id=KERNEL_ID, has_side_effects=True, vmem_limit_bytes=VMEM_BYTES
        ),
    )(*flat_in)
    done = types.SimpleNamespace(**jax.tree.unflatten(out_tree, flat_out))

    def unpadded(rows, half):
        outs = []
        for group in range(2):
            image, width = by_group[group], rows.shape[1]
            across, side = (8, image.half_side) if half else (16, image.side)
            start = image.half_at if half else image.at
            count = image.half_count if half else image.count
            part = rows[start : start + counts[group] * count].reshape(counts[group], count // across, across, width)
            outs.append(part[:, :side, :side])
        return outs

    me = lax.axis_index("dp")
    outs = unpadded(done.out, True) + unpadded(done.dinput, False)
    at = 0
    for k, grad in enumerate(done.dfilter):
        if spare > 1:
            grad = lax.psum_scatter(grad.astype(F32), "dp", axis_index_groups=spare_groups(spare), tiled=True)
        share = wide[k] // devices
        affine = lax.dynamic_slice(done.daffine, (0, at + me * share), (2, share)).T
        outs += [grad.astype(F32), affine]
        at += wide[k]
    return tuple(outs)


VMEM_BYTES = 65400 * 1024


def solution(mesh):
    images = P(("dp", "outer"), None, None, None)
    rows = P("dp", None)
    return jax.shard_map(
        local,
        mesh=mesh,
        in_specs=(images, images, P(("dp", "outer")), P(("dp", "outer")), images, images) + (rows,) * 14,
        out_specs=(images,) * 4 + (rows,) * 14,
        check_vma=False,
    )
```

profile of v0, /device:TPU:1, one launch (start us, length us, event | category | flops | bytes accessed | tf_op | source)
XLA Modules:
  0.0 262.9 jit_solution(883417374757421297)
XLA Ops:
  0.7 1.0 copy.59
  1.7 0.1 pad.25.clone
  1.7 0.0 copy-start.16
  1.7 0.0 copy-start.17
  1.8 0.0 copy-start.18
  1.8 0.0 copy-start.10
  1.8 0.0 copy-start.11
  1.8 0.0 copy-start.12
  1.8 0.0 copy-start.13
  1.8 0.0 copy-start.14
  1.8 0.0 copy-start.15
  1.8 0.0 copy-start.2
  1.9 1.2 copy.58
  3.1 0.1 pad.24.clone
  3.2 0.0 copy-start.1
  3.2 1.0 pad_maximum_fusion.1.flat_0_
  4.2 0.0 copy-done.16
  4.2 0.1 pad_add_fusion
  4.3 0.1 fusion
  4.3 0.1 reshape.91
  4.4 0.7 broadcast_in_dim.2.flat_1_
  5.2 0.1 concatenate.14
  5.3 0.6 pad.27.flat_9_
  5.9 0.1 copy.61
  6.0 0.1 pad.29.clone
  6.1 0.2 copy.60
  6.3 0.1 pad.28.clone
  6.5 1.4 pad_maximum_fusion.flat_10_
  7.8 237.3 %shard_map.331 = (f32[8,6656]{1,0:T(8,128)}, bf16[64,256]{1,0:T(8,128)(2,1)}, bf16[144,256]{1,0:T(8,128)(2,1)}, bf16[16,1024]{1,0:T(8,128)(2,1)}, bf16[64,512]{1...) custom-call(bf16[224,2048]{1,0:T(8,128)(2,1)} %pad_maximum_fusion.1., ...), custom_call_target="tpu_custom_call" | custom-call | tf_op jit(solution)/shard_map/pallas_call | solution.py:1314
  245.1 1.1 slice.24
  246.2 1.2 copy.54
  247.4 1.0 slice.26
  248.5 0.9 copy.55
  249.4 0.1 slice.28
  249.5 0.1 slice.34
  249.5 1.7 copy.56
  251.4 1.2 copy.57
  252.6 0.6 convert_element_type.45
  253.2 1.3 fusion.2
  254.6 0.7 convert_element_type.46
  255.2 0.6 convert_element_type.47
  255.9 1.3 fusion.3
  257.2 0.7 convert_element_type.48
  257.9 1.3 fusion.5
  259.2 0.9 convert_element_type.49
  260.1 0.7 convert_element_type.50
  260.8 1.3 fusion.7
  262.0 0.8 convert_element_type.51
  (32 shorter events, 0.2 us)
Async XLA Ops:
  1.7 2.5 copy-start.16
  1.7 2.4 copy-start.17
  1.8 3.3 %copy-start.18 = (bf16[32,2]{0,1:T(2,128)(2,1)S(1)}, bf16[32,2]{0,1:T(2,128)(2,1)}, u32[]{:S(2)}) copy-start(bf16[32,2]{0,1:T(2,128)(2,1)} %param.35) | copy-start | bytes 388
  1.8 3.3 %copy-start.10 = (bf16[16,2]{0,1:T(2,128)(2,1)S(1)}, bf16[16,2]{0,1:T(2,128)(2,1)}, u32[]{:S(2)}) copy-start(bf16[16,2]{0,1:T(2,128)(2,1)} %param.27) | copy-start | bytes 196
  1.8 3.3 %copy-start.11 = (bf16[16,2]{0,1:T(2,128)(2,1)S(1)}, bf16[16,2]{0,1:T(2,128)(2,1)}, u32[]{:S(2)}) copy-start(bf16[16,2]{0,1:T(2,128)(2,1)} %param.29) | copy-start | bytes 196
  1.8 3.3 %copy-start.12 = (bf16[64,2]{0,1:T(2,128)(2,1)S(1)}, bf16[64,2]{0,1:T(2,128)(2,1)}, u32[]{:S(2)}) copy-start(bf16[64,2]{0,1:T(2,128)(2,1)} %param.31) | copy-start | bytes 772
  1.8 3.3 %copy-start.13 = (bf16[32,2]{0,1:T(2,128)(2,1)S(1)}, bf16[32,2]{0,1:T(2,128)(2,1)}, u32[]{:S(2)}) copy-start(bf16[32,2]{0,1:T(2,128)(2,1)} %param.33) | copy-start | bytes 388
  1.8 3.3 %copy-start.14 = (bf16[128,2]{0,1:T(2,128)(2,1)S(1)}, bf16[128,2]{0,1:T(2,128)(2,1)}, u32[]{:S(2)}) copy-start(bf16[128,2]{0,1:T(2,128)(2,1)} %param.37) | copy-start | bytes 1540
  1.8 3.3 %copy-start.15 = (bf16[128,2]{0,1:T(2,128)(2,1)S(1)}, bf16[128,2]{0,1:T(2,128)(2,1)}, u32[]{:S(2)}) copy-start(bf16[128,2]{0,1:T(2,128)(2,1)} %param.39) | copy-start | bytes 1540
  1.8 4.0 %copy-start.2 = (bf16[2,10,10,1024]{3,0,2,1:T(2,128)(2,1)S(1)}, bf16[2,10,10,1024]{3,0,2,1:T(2,128)(2,1)}, u32[]{:S(2)}) copy-start(bf16[2,10,10,1024]{3,0,2,1:T(2,128)(2,1)} %param.21) | copy-start | bytes 1228804
  3.2 2.9 %copy-start.1 = (bf16[2,14,14,1024]{3,0,2,1:T(2,128)(2,1)S(1)}, bf16[2,14,14,1024]{3,0,2,1:T(2,128)(2,1)}, u32[]{:S(2)}) copy-start(bf16[2,14,14,1024]{3,0,2,1:T(2,128)(2,1)} %param.20) | copy-start | bytes 2408452
  246.2 3.2 %copy-start = (bf16[832,1024]{1,0:T(8,128)(2,1)S(1)}, bf16[832,1024]{1,0:T(8,128)(2,1)}, u32[]{:S(2)}) copy-start(bf16[832,1024]{1,0:T(8,128)(2,1)} %get-tuple-element.29) | copy-start | bytes 5111812
  251.3 1.3 copy-start.9
  251.3 3.3 %copy-start.6 = (bf16[144,256]{1,0:T(8,128)(2,1)S(1)}, bf16[144,256]{1,0:T(8,128)(2,1)}, u32[]{:S(2)}) copy-start(bf16[144,256]{1,0:T(8,128)(2,1)} %get-tuple-element.32) | copy-start | bytes 221188
  251.3 3.9 %copy-start.8 = (bf16[16,1024]{1,0:T(8,128)(2,1)S(1)}, bf16[16,1024]{1,0:T(8,128)(2,1)}, u32[]{:S(2)}) copy-start(bf16[16,1024]{1,0:T(8,128)(2,1)} %get-tuple-element.33) | copy-start | bytes 98308
  251.3 5.9 %copy-start.7 = (bf16[64,512]{1,0:T(8,128)(2,1)S(1)}, bf16[64,512]{1,0:T(8,128)(2,1)}, u32[]{:S(2)}) copy-start(bf16[64,512]{1,0:T(8,128)(2,1)} %get-tuple-element.34) | copy-start | bytes 196612
  251.3 7.8 %copy-start.3 = (bf16[288,512]{1,0:T(8,128)(2,1)S(1)}, bf16[288,512]{1,0:T(8,128)(2,1)}, u32[]{:S(2)}) copy-start(bf16[288,512]{1,0:T(8,128)(2,1)} %get-tuple-element.35) | copy-start | bytes 884740
  251.3 8.7 %copy-start.5 = (bf16[32,2048]{1,0:T(8,128)(2,1)S(1)}, bf16[32,2048]{1,0:T(8,128)(2,1)}, u32[]{:S(2)}) copy-start(bf16[32,2048]{1,0:T(8,128)(2,1)} %get-tuple-element.36) | copy-start | bytes 393220
  251.4 10.6 %copy-start.4 = (bf16[64,2048]{1,0:T(8,128)(2,1)S(1)}, bf16[64,2048]{1,0:T(8,128)(2,1)}, u32[]{:S(2)}) copy-start(bf16[64,2048]{1,0:T(8,128)(2,1)} %get-tuple-element.37) | copy-start | bytes 786436
where the time goes:
time: 263 us
  Pallas kernels  237 us (90%)
  local copies, waits for them, and re-layouts  17.1 us (7%)
  other arithmetic  7.59 us (3%)
    pallas_call x1, Pallas kernels, local(): pl.pallas_call(kernel, out_shape=flat_out, in_specs=[pl.BlockSpec(memory_...  237 us
    unnamed x46, local copies, waits for them, and re-layouts  7.65 us

commit v1 on v0

--- a/solution.py
+++ b/solution.py
@@ -83,12 +83,12 @@
         self.refs = refs
 
     @staticmethod
-    def scratch(rows, width, spare, split):
+    def scratch(rows, width, spare, split, kind=F32):
         piece = width // 2 if split else width
         shapes = []
         for count in Reduce.counts(spare, split):
-            shapes.append(pltpu.VMEM((count, rows, piece), F32))
-            shapes.append(pltpu.VMEM((rows, piece), F32))
+            shapes.append(pltpu.VMEM((count, rows, piece), kind))
+            shapes.append(pltpu.VMEM((rows, piece), kind))
         phases = len(Reduce.counts(spare, split))
         shapes.append(pltpu.SemaphoreType.DMA((phases + 1,)))
         shapes.append(pltpu.SemaphoreType.DMA((phases + 1,)))
@@ -122,14 +122,14 @@
             if between is not None:
                 between(p)
             await_bytes(slots, recv_sem.at[p])
-            value = src[:, mine] if crossing else held[...]
+            value = (src[:, mine] if crossing else held[...]).astype(F32)
             for k in range(len(devices)):
-                value = value + slots[k]
+                value = value + slots[k].astype(F32)
             last = p == len(phases) - 1 and not split
             if last:
                 out[...] = value
             else:
-                total[...] = value
+                total[...] = value.astype(total.dtype)
             held = total
         if split:
             send(held, out.at[:, mine], send_sem.at[len(phases)], recv_sem.at[len(phases)], place.sibling())
@@ -244,17 +244,20 @@
             pltpu.VMEM((3, rows, half), BF16),
         ]
 
+    def stretch(self):
+        rows = self.landing[2].shape[1]
+        width = 512 if rows < 64 else 256 if rows < 128 else 128
+        return min(width, self.half)
+
     def add(self, near, block):
-        blocks = self.half // 128
+        width = self.stretch()
         whole, base, rows = self.whole, self.base, self.rows
 
-        @pl.loop(0, 4 * blocks)
-        def _(i):
-            far, b = lax.div(i, blocks), lax.rem(i, blocks)
-            here = pl.ds(pl.multiple_of(base + b * 128, 128), 128)
-            there = pl.ds(pl.multiple_of(b * 128, 128), 128)
-            total = whole[far, near, rows, here].astype(F32) + block[far, :, there].astype(F32)
-            whole[far, near, rows, here] = total.astype(BF16)
+        @pl.loop(0, self.half // width)
+        def _(b):
+            here = pl.ds(pl.multiple_of(base + b * width, 128), width)
+            there = pl.ds(pl.multiple_of(b * width, 128), width)
+            whole[:, near, rows, here] = whole[:, near, rows, here] + block[:, :, there]
 
     def start(self):
         send(
@@ -268,17 +271,16 @@
     def second(self):
         place = self.place
         await_bytes(self.landing[0], self.recv_sem.at[0])
-        blocks = self.half // 128
+        width = self.stretch()
         whole, base, rows, block = self.whole, self.base, self.rows, self.landing[0]
-
-        @pl.loop(0, 16 * blocks)
+        strips = self.half // width
+
+        @pl.loop(0, 4 * strips)
         def _(i):
-            group, b = lax.div(i, blocks), lax.rem(i, blocks)
-            far, near = lax.div(group, 4), lax.rem(group, 4)
-            here = pl.ds(pl.multiple_of(base + b * 128, 128), 128)
-            there = pl.ds(pl.multiple_of(b * 128, 128), 128)
-            total = whole[far, near, rows, here].astype(F32) + block[far, near, :, there].astype(F32)
-            whole[far, near, rows, here] = total.astype(BF16)
+            near, b = lax.div(i, strips), lax.rem(i, strips)
+            here = pl.ds(pl.multiple_of(base + b * width, 128), width)
+            there = pl.ds(pl.multiple_of(b * width, 128), width)
+            whole[:, near, rows, here] = whole[:, near, rows, here] + block[:, near, :, there]
 
         if self.direct:
             landings = (self.landing[1].at[0], self.landing[1].at[1], self.landing[2])
@@ -544,10 +546,17 @@
                 if during is not None:
                     during(p)
 
-        slots = refs.slots[way if k in (NARROW, LAST) else 0][k]
-        Reduce(place, k == LAST, list(slots) + list(refs.sums_sem[way][k])).run(
-            refs.given[way][k], refs.total[way][k], between
-        )
+        given, total = refs.given[way][k], refs.total[way][k]
+        run = Reduce(place, k == LAST, list(refs.slots[way][k]) + list(refs.sums_sem[way][k])).run
+        if way == 0:
+            run(given, total, between)
+        else:
+            half = given.shape[1] // 2
+            packed, summed = refs.packed[k], refs.summed[k]
+            packed[...] = jnp.concatenate([given[:, 0:half], given[:, half:]], axis=0).astype(BF16)
+            run(packed, summed, between)
+            value = summed[...].astype(F32)
+            total[:, 0:half], total[:, half:] = value[0:8], value[8:16]
         point()
 
     def hot_row(image, view):
@@ -1068,9 +1077,11 @@
     def during(p):
         if p == 0:
             let_go(SPATIAL)
-            for r in range(3):
+        if p < 2:
+            for r in ((0, 1), (2,))[p]:
                 value = mul(taps1[16 * r : 16 * r + full_rows, :], grad3[16 : 16 + full_rows, mid1 : 2 * mid1], TN)
                 store_piece(whole[SPATIAL], r * 3 * mid1, value.astype(BF16))
+        if p == 1:
             send_off(SPATIAL)
 
     point()
@@ -1154,7 +1165,8 @@
     17: [(FORWARD, E0), (NEAR, E1), (BEGIN, B1)],
     18: [(CROSS, T3, E0)],
     19: [(NEAR, B0), (BEGIN, B2)],
-    22: [(FORWARD, E1, B0), (NEAR, B1), (BEGIN, B3)],
+    21: [(BEGIN, B3)],
+    22: [(FORWARD, E1, B0), (NEAR, B1)],
     23: [(CROSS, E1, B0)],
     24: [(NEAR, B2), (FORWARD, B1)],
     25: [(NEAR, B3), (FORWARD, B2), (CROSS, B1)],
@@ -1175,9 +1187,11 @@
     52: [(R5, B1, B2)],
     53: [(R2, K), (R3, T3), (R4, T2)],
     54: [(R2, W)],
-    56: [(R3, K, W), (R4, T3)],
-    57: [(R5, B3, T0, T1), (R2, S)],
-    58: [(R3, S), (R4, K, W)],
+    55: [(R3, W)],
+    56: [(R3, K), (R4, T3)],
+    57: [(R5, B3, T0, T1)],
+    58: [(R2, S), (R4, K, W)],
+    59: [(R3, S)],
     60: [(R4, S), (R5, T2, T3)],
     61: [(R5, K, W)],
     62: [(R2, N)],
@@ -1209,7 +1223,7 @@
     filters, affines = params[0::2], params[1::2]
     devices = lax.axis_size("dp")
     spare = devices // 16
-    inputs, cotans, views = (input_big, input_small), (cotan_big, cotan_small), (views_big, views_small)
+    inputs, cotans = (input_big, input_small), (cotan_big, cotan_small)
     counts = [item.shape[0] for item in inputs]
     images, full_rows, half_rows = images_of(counts, [item.shape[1] for item in inputs])
     c_in, c_out = input_big.shape[3], cotan_big.shape[3]
@@ -1219,7 +1233,7 @@
     by_group = [next(image for image in images if image.group == g) for g in range(2)]
     x = jnp.concatenate([padded(inputs[g], by_group[g].count // 16, 16) for g in range(2)])
     cot = jnp.concatenate([padded(cotans[g], by_group[g].half_count // 8, 8) for g in range(2)])
-    view = jnp.concatenate(views)
+    view = jnp.concatenate([views_big, views_small])
     hot = (view[:, None] == jnp.arange(2, dtype=jnp.int32)[None, :]).astype(F32)
     hot = jnp.broadcast_to(hot.reshape(-1, 1), (2 * len(images), 128))
 
@@ -1253,9 +1267,10 @@
 
     rounds = [wide[:5] + [2 * c_out], wide[:5] + [2 * c_out]]
     rounds[0][NARROW] += 128
-    sums = [[Reduce.scratch(8, width, spare, k == LAST) for k, width in enumerate(way)] for way in rounds]
-    slots = [[item[:-2] for item in way] for way in sums]
-    slots[1] = [item if k in (NARROW, LAST) else [] for k, item in enumerate(slots[1])]
+    sums = [
+        [Reduce.scratch(8, width, spare, k == LAST) for k, width in enumerate(rounds[0])],
+        [Reduce.scratch(16, width // 2, spare, k == LAST, BF16) for k, width in enumerate(rounds[1])],
+    ]
     operands = dict(x=x, cot=cot, hot=hot, shards=shards)
     results = dict(
         out=jax.ShapeDtypeStruct((half_rows, c_out), BF16),
@@ -1291,7 +1306,9 @@
         even=rounded(half_rows, c_in),
         given=[[field(8, width) for width in way] for way in rounds],
         total=[[field(8, width) for width in way] for way in rounds],
-        slots=slots,
+        slots=[[item[:-2] for item in way] for way in sums],
+        packed=[rounded(16, width // 2) for width in rounds[1]],
+        summed=[(rounded if k == LAST else field)(16, width // 2) for k, width in enumerate(rounds[1])],
         sums_sem=[[item[-2:] for item in way] for way in sums],
         load_sem=pltpu.SemaphoreType.DMA((len(PIECES) + 3,)),
         store_sem=pltpu.SemaphoreType.DMA((16,)),
@@ -1323,28 +1340,59 @@
     )(*flat_in)
     done = types.SimpleNamespace(**jax.tree.unflatten(out_tree, flat_out))
 
-    def unpadded(rows, half):
-        outs = []
-        for group in range(2):
-            image, width = by_group[group], rows.shape[1]
-            across, side = (8, image.half_side) if half else (16, image.side)
+    shares = [width // devices for width in wide]
+    views = [(group, half) for half in (True, False) for group in range(2)]
+
+    def image_shape(group, half):
+        side = by_group[group].half_side if half else by_group[group].side
+        return counts[group], side, side, c_out if half else c_in
+
+    def finish(*flat):
+        given, images_out, grads_out, affine_out = flat[:10], flat[10:14], flat[14:21], flat[21:28]
+        held, sem = flat[28:38], flat[38]
+        copies = [pltpu.make_async_copy(given[k], held[k], sem.at[k]) for k in range(10)]
+        for copy in copies:
+            copy.start()
+        for copy in copies:
+            copy.wait()
+        out, dinput, daffine, *grads = held
+        for ref, (group, half) in zip(images_out, views):
+            image, rows = by_group[group], out if half else dinput
             start = image.half_at if half else image.at
             count = image.half_count if half else image.count
-            part = rows[start : start + counts[group] * count].reshape(counts[group], count // across, across, width)
-            outs.append(part[:, :side, :side])
-        return outs
-
-    me = lax.axis_index("dp")
-    outs = unpadded(done.out, True) + unpadded(done.dinput, False)
-    at = 0
-    for k, grad in enumerate(done.dfilter):
+            across = 8 if half else 16
+            number, side, _, width = ref.shape
+            for n in range(number):
+                for row in range(side):
+                    here = start + n * count + row * across
+                    ref[n, row] = rows[here : here + across, :][:side]
+        for ref, grad in zip(grads_out, grads):
+            ref[...] = grad[...].astype(F32)
+        me, at = lax.axis_index("dp"), 0
+        for k, ref in enumerate(affine_out):
+            first = me * shares[k]
+            block, shift = lax.div(first, 128), lax.rem(first, 128)
+            rows = daffine[:, pl.ds(pl.multiple_of(at + block * 128, 128), 128)]
+            ref[...] = pltpu.roll(rows, lax.rem(128 - shift, 128), 1)[0:2, 0 : shares[k]]
+            at += wide[k]
+
+    finals = [done.out, done.dinput, done.daffine, *done.dfilter]
+    outs = pl.pallas_call(
+        finish,
+        out_shape=[jax.ShapeDtypeStruct(image_shape(*view), BF16) for view in views]
+        + [jax.ShapeDtypeStruct(shape, F32) for shape in shapes[:7]]
+        + [jax.ShapeDtypeStruct((2, share), F32) for share in shares],
+        in_specs=[pl.BlockSpec(memory_space=pl.ANY)] * 10,
+        out_specs=[pl.BlockSpec(memory_space=pltpu.VMEM)] * 18,
+        scratch_shapes=[pltpu.VMEM(item.shape, item.dtype) for item in finals] + [pltpu.SemaphoreType.DMA((10,))],
+        compiler_params=pltpu.CompilerParams(vmem_limit_bytes=VMEM_BYTES),
+    )(*finals)
+    results = list(outs[:4])
+    for grad, affine in zip(outs[4:11], outs[11:]):
         if spare > 1:
-            grad = lax.psum_scatter(grad.astype(F32), "dp", axis_index_groups=spare_groups(spare), tiled=True)
-        share = wide[k] // devices
-        affine = lax.dynamic_slice(done.daffine, (0, at + me * share), (2, share)).T
-        outs += [grad.astype(F32), affine]
-        at += wide[k]
-    return tuple(outs)
+            grad = lax.psum_scatter(grad, "dp", axis_index_groups=spare_groups(spare), tiled=True)
+        results += [grad, affine.T]
+    return tuple(results)
 
 
 VMEM_BYTES = 65400 * 1024

time: 263 us -> 249 us (0.947)
  Pallas kernels: 237 us -> 230 us
  other arithmetic: 7.59 us -> 3.18 us
  local copies, waits for them, and re-layouts: 17.1 us -> 14 us
    pallas_call x1, Pallas kernels: 237 us -> 226 us  [local(): pl.pallas_call(kernel, out_shape=flat_out, in_specs=[pl.BlockSpec(memory_...]
    transpose x4 -> x0, local copies, waits for them, and re-layouts: 5.21 us -> none  [local(): affine = lax.dynamic_slice(done.daffine, (0, at + me * share), (2, share)).T]
    convert_element_type x7 -> x0, other arithmetic: 5.04 us -> none  [local(): outs += [grad.astype(F32), affine]]
    pallas_call x0 -> x1, Pallas kernels: none -> 4.18 us  [local(): pl.pallas_call(finish, out_shape=[jax.ShapeDtypeStruct(image_shape(*view)...]
    unnamed x46 -> x14, local copies, waits for them, and re-layouts: 7.65 us -> 10.8 us
where the time goes in v1:
time: 249 us; the launch traced here: 248 us
  Pallas kernels  230 us (92%)
  local copies, waits for them, and re-layouts  14 us (6%)
  other arithmetic  3.18 us (1%)
    pallas_call x1, Pallas kernels, local(): pl.pallas_call(kernel, out_shape=flat_out, in_specs=[pl.BlockSpec(memory_...  226 us
    unnamed x14, local copies, waits for them, and re-layouts  10.8 us

profile of v1, /device:TPU:1, one launch (start us, length us, event | category | flops | bytes accessed | tf_op | source)
XLA Modules:
  0.0 248.3 jit_solution(17358933919037730579)
XLA Ops:
  0.7 0.7 pad_add_fusion
  1.4 0.7 pad.26
  2.1 0.8 concatenate.14
  2.9 0.1 fusion
  3.0 0.1 reshape.75
  3.1 0.6 pad.27.flat_9_
  3.7 0.7 broadcast_in_dim.2.flat_1_
  4.3 1.0 copy.55
  5.3 0.1 pad.25.clone
  5.4 0.0 copy-start.2
  5.4 1.2 copy.54
  6.6 0.1 pad.24.clone
  6.7 0.0 copy-start.1
  6.7 1.0 pad_maximum_fusion.1.flat_0_
  7.8 0.0 copy-done.2
  7.8 0.1 copy.57
  7.9 0.1 pad.29.clone
  8.0 0.1 copy-done.1
  8.1 0.2 copy.56
  8.3 0.1 pad.28.clone
  8.5 1.3 pad_maximum_fusion.flat_10_
  9.8 226.1 %shard_map.331 = (f32[8,6656]{1,0:T(8,128)}, bf16[64,256]{1,0:T(8,128)(2,1)}, bf16[144,256]{1,0:T(8,128)(2,1)}, bf16[16,1024]{1,0:T(8,128)(2,1)}, bf16[64,512]{1...) custom-call(bf16[224,2048]{1,0:T(8,128)(2,1)} %pad_maximum_fusion.1., ...), custom_call_target="tpu_custom_call" | custom-call | tf_op jit(solution)/shard_map/pallas_call | solution.py:1331
  235.9 4.2 %shard_map.332 = (bf16[2,7,7,2048]{3,2,1,0:T(8,128)(2,1)}, bf16[2,5,5,2048]{3,2,1,0:T(8,128)(2,1)}, bf16[2,14,14,1024]{3,2,1,0:T(8,128)(2,1)}, bf16[2,10,10,1024...) custom-call(bf16[224,2048]{1,0:T(8,128)(2,1)} %get-tuple-element.46., ...), custom_call_target="tpu_custom_call" | custom-call | tf_op jit(solution)/shard_map/pallas_call | solution.py:1380
  240.1 0.0 copy-start
  240.1 2.3 copy.50
  242.4 1.9 copy.51
  244.3 2.3 copy.53
  246.5 0.0 copy-done
  246.5 1.7 copy.52
  (1 shorter events, 0.0 us)
Async XLA Ops:
  5.4 2.4 copy-start.2
  6.7 1.4 copy-start.1
  240.1 6.4 %copy-start = (bf16[2,14,14,1024]{3,2,1,0:T(8,128)(2,1)S(1)}, bf16[2,14,14,1024]{3,2,1,0:T(8,128)(2,1)}, u32[]{:S(2)}) copy-start(bf16[2,14,14,1024]{3,2,1,0:T(8,128)(2,1)} %get-tuple-element.94) | copy-start | bytes 2408452

commit v2 on v1

--- a/solution.py
+++ b/solution.py
@@ -1143,60 +1143,49 @@
 NEAR, FORWARD, CROSS = GATHER_STEPS
 R2, R3, R4, R5 = Scatter.second, Scatter.first, Scatter.fars, Scatter.cross
 PLAN = {
-    0: [
-        (BEGIN, TAB, N),
-        (NEAR, TAB, N),
-        (BEGIN, S, W, K, T0),
-        (FORWARD, TAB, N),
-        (CROSS, N),
-        (NEAR, S),
-    ],
-    1: [(CROSS, TAB)],
-    2: [(FORWARD, S), (NEAR, W, K), (BEGIN, T1)],
+    0: [(BEGIN, TAB, N, S, W, K, T0), (NEAR, TAB, N, S), (FORWARD, TAB, N), (CROSS, N)],
+    1: [(CROSS, TAB), (BEGIN, T1)],
+    2: [(FORWARD, S), (NEAR, W, K), (BEGIN, T2)],
     3: [(CROSS, S)],
-    4: [(FORWARD, W), (NEAR, T0), (BEGIN, T2)],
+    4: [(FORWARD, W), (NEAR, T0), (BEGIN, T3)],
     6: [(CROSS, W)],
-    7: [(FORWARD, K, T0), (NEAR, T1), (BEGIN, T3)],
+    7: [(FORWARD, K, T0), (NEAR, T1), (BEGIN, E0)],
     8: [(CROSS, K, T0)],
-    9: [(NEAR, T2), (BEGIN, E0)],
-    12: [(FORWARD, T1, T2), (NEAR, T3), (BEGIN, E1)],
+    9: [(NEAR, T2), (BEGIN, E1)],
+    12: [(FORWARD, T1, T2), (NEAR, T3), (BEGIN, B0)],
     13: [(CROSS, T1, T2)],
-    14: [(NEAR, E0), (FORWARD, T3), (BEGIN, B0)],
-    17: [(FORWARD, E0), (NEAR, E1), (BEGIN, B1)],
+    14: [(NEAR, E0), (FORWARD, T3), (BEGIN, B1)],
+    17: [(FORWARD, E0), (NEAR, E1, B0), (BEGIN, B2)],
     18: [(CROSS, T3, E0)],
-    19: [(NEAR, B0), (BEGIN, B2)],
-    21: [(BEGIN, B3)],
-    22: [(FORWARD, E1, B0), (NEAR, B1)],
-    23: [(CROSS, E1, B0)],
-    24: [(NEAR, B2), (FORWARD, B1)],
-    25: [(NEAR, B3), (FORWARD, B2), (CROSS, B1)],
-    26: [(FORWARD, B3), (CROSS, B2, B3)],
+    19: [(FORWARD, E1), (NEAR, B1), (BEGIN, B3)],
+    22: [(FORWARD, B0, B1), (NEAR, B2, B3)],
+    23: [(CROSS, E1, B0, B1)],
+    24: [(FORWARD, B2)],
+    25: [(FORWARD, B3)],
+    26: [(CROSS, B2, B3)],
     37: [(R2, E0, E1)],
     38: [(R2, B0)],
     39: [(R3, E0, E1), (R2, B1)],
     40: [(R4, E0)],
-    41: [(R3, B0, B1), (R2, B2), (R4, E1)],
+    41: [(R3, B0, B1), (R2, B2, B3), (R4, E1)],
     42: [(R5, E0)],
-    43: [(R2, B3), (R3, B2), (R4, B0)],
-    44: [(R2, T0), (R4, B1)],
-    46: [(R3, B3, T0), (R2, T1), (R4, B2)],
+    43: [(R3, B2), (R4, B0)],
+    46: [(R3, B3), (R2, T0, T1), (R4, B1, B2)],
     47: [(R5, E1, B0)],
-    48: [(R2, T2), (R4, B3)],
+    48: [(R3, T0), (R4, B3)],
     49: [(R3, T1), (R4, T0)],
-    51: [(R3, T2), (R2, T3), (R4, T1)],
+    51: [(R2, T2, T3), (R4, T1)],
     52: [(R5, B1, B2)],
-    53: [(R2, K), (R3, T3), (R4, T2)],
-    54: [(R2, W)],
-    55: [(R3, W)],
-    56: [(R3, K), (R4, T3)],
+    53: [(R2, K), (R3, T2)],
+    54: [(R3, T3)],
+    56: [(R3, K), (R2, W), (R4, T2)],
     57: [(R5, B3, T0, T1)],
-    58: [(R2, S), (R4, K, W)],
-    59: [(R3, S)],
+    58: [(R2, S), (R3, W), (R4, K, T3)],
+    59: [(R3, S), (R4, W)],
     60: [(R4, S), (R5, T2, T3)],
-    61: [(R5, K, W)],
-    62: [(R2, N)],
-    63: [(R5, S)],
-    65: [(R3, N), (R4, N), (R5, N)],
+    61: [(R2, N), (R5, K, W)],
+    63: [(R3, N), (R4, N), (R5, S)],
+    65: [(R5, N)],
 }
 
 

time: 249 us -> 236 us (0.948)
  Pallas kernels: 230 us -> 218 us
    pallas_call x1, Pallas kernels: 226 us -> 214 us  [local(): pl.pallas_call(kernel, out_shape=flat_out, in_specs=[pl.BlockSpec(memory_...]
where the time goes in v2:
time: 236 us
  Pallas kernels  218 us (92%)
  local copies, waits for them, and re-layouts  14 us (6%)
  other arithmetic  3.18 us (1%)
    pallas_call x1, Pallas kernels, local(): pl.pallas_call(kernel, out_shape=flat_out, in_specs=[pl.BlockSpec(memory_...  214 us
    unnamed x14, local copies, waits for them, and re-layouts  10.8 us

profile of v2, /device:TPU:1, one launch (start us, length us, event | category | flops | bytes accessed | tf_op | source)
XLA Modules:
  0.0 236.0 jit_solution(2207737514539617607)
XLA Ops:
  0.7 0.7 pad_add_fusion
  1.4 0.7 pad.26
  2.1 0.8 concatenate.14
  2.9 0.1 fusion
  3.0 0.1 reshape.75
  3.1 0.6 pad.27.flat_9_
  3.7 0.7 broadcast_in_dim.2.flat_1_
  4.3 1.0 copy.55
  5.3 0.1 pad.25.clone
  5.4 0.0 copy-start.2
  5.4 1.2 copy.54
  6.6 0.1 pad.24.clone
  6.7 0.0 copy-start.1
  6.7 1.0 pad_maximum_fusion.1.flat_0_
  7.8 0.0 copy-done.2
  7.8 0.1 copy.57
  7.9 0.1 pad.29.clone
  8.0 0.1 copy-done.1
  8.1 0.2 copy.56
  8.3 0.1 pad.28.clone
  8.5 1.3 pad_maximum_fusion.flat_10_
  9.8 213.9 %shard_map.331 = (f32[8,6656]{1,0:T(8,128)}, bf16[64,256]{1,0:T(8,128)(2,1)}, bf16[144,256]{1,0:T(8,128)(2,1)}, bf16[16,1024]{1,0:T(8,128)(2,1)}, bf16[64,512]{1...) custom-call(bf16[224,2048]{1,0:T(8,128)(2,1)} %pad_maximum_fusion.1., ...), custom_call_target="tpu_custom_call" | custom-call | tf_op jit(solution)/shard_map/pallas_call | solution.py:1320
  223.7 4.2 %shard_map.332 = (bf16[2,7,7,2048]{3,2,1,0:T(8,128)(2,1)}, bf16[2,5,5,2048]{3,2,1,0:T(8,128)(2,1)}, bf16[2,14,14,1024]{3,2,1,0:T(8,128)(2,1)}, bf16[2,10,10,1024...) custom-call(bf16[224,2048]{1,0:T(8,128)(2,1)} %get-tuple-element.46., ...), custom_call_target="tpu_custom_call" | custom-call | tf_op jit(solution)/shard_map/pallas_call | solution.py:1369
  227.9 0.0 copy-start
  227.9 2.3 copy.50
  230.2 1.9 copy.51
  232.0 2.3 copy.53
  234.3 0.0 copy-done
  234.3 1.7 copy.52
  (1 shorter events, 0.0 us)
Async XLA Ops:
  5.4 2.4 copy-start.2
  6.7 1.4 copy-start.1
  227.9 6.4 %copy-start = (bf16[2,14,14,1024]{3,2,1,0:T(8,128)(2,1)S(1)}, bf16[2,14,14,1024]{3,2,1,0:T(8,128)(2,1)}, u32[]{:S(2)}) copy-start(bf16[2,14,14,1024]{3,2,1,0:T(8,128)(2,1)} %get-tuple-element.94) | copy-start | bytes 2408452

commit v3 on v2

--- a/solution.py
+++ b/solution.py
@@ -109,7 +109,7 @@
             mine = pl.ds(pl.multiple_of(place.core * piece, 128), piece)
             other = pl.ds(pl.multiple_of((1 - place.core) * piece, 128), piece)
         else:
-            phases = [[place.sibling()] + place.nears() + place.cross_nears(), place.fars()]
+            phases = [place.cross_nears() + place.nears() + [place.sibling()], place.fars()]
         if place.spare > 1:
             phases.append(place.rests())
         held = src
@@ -483,7 +483,6 @@
         )
         for item in gathers
     ]
-    load_hot = load(refs.hot, hot)
     load_x = load(refs.x, refs.x_v)
     load_cot = load(refs.cot, refs.cot_v)
     scatters = [
@@ -531,6 +530,14 @@
                     step(gathers[k] if step in GATHER_STEPS else scatters[k])
 
     greet([place.sibling()] + place.nears() + place.cross_nears() + place.fars() + place.rests())
+
+    at = [0, 0]
+    for image in images:
+        seen = refs.views[image.group][at[image.group]].astype(F32)
+        at[image.group] += 1
+        row = 2 * image.index
+        hot[row : row + 1, :] = jnp.full((1, 128), 1.0 - seen)
+        hot[row + 1 : row + 2, :] = jnp.full((1, 128), seen)
 
     layers, lane = [], 0
     for k, width in enumerate(widths_of(*widths)):
@@ -712,7 +719,6 @@
                 mine = jnp.where(lax.div(b * 128 + to, share) == owner, spread, 0.0)
                 layer.affine[kind : kind + 1, b * 128 : (b + 1) * 128] = column_sum(mine)
 
-    load_hot.wait()
     load_x.wait()
     point()
 
@@ -1009,7 +1015,7 @@
         put_sums(refs.given[1][SHRINK], cols, firsts, seconds)
 
     def during(p):
-        if p == 0:
+        if p == 1:
             filter_grad(STRIDE, taps2, stride_grad, 1)
             send_off(STRIDE)
 
@@ -1078,7 +1084,7 @@
         if p == 0:
             let_go(SPATIAL)
         if p < 2:
-            for r in ((0, 1), (2,))[p]:
+            for r in ((0,), (1, 2))[p]:
                 value = mul(taps1[16 * r : 16 * r + full_rows, :], grad3[16 : 16 + full_rows, mid1 : 2 * mid1], TN)
                 store_piece(whole[SPATIAL], r * 3 * mid1, value.astype(BF16))
         if p == 1:
@@ -1222,9 +1228,6 @@
     by_group = [next(image for image in images if image.group == g) for g in range(2)]
     x = jnp.concatenate([padded(inputs[g], by_group[g].count // 16, 16) for g in range(2)])
     cot = jnp.concatenate([padded(cotans[g], by_group[g].half_count // 8, 8) for g in range(2)])
-    view = jnp.concatenate([views_big, views_small])
-    hot = (view[:, None] == jnp.arange(2, dtype=jnp.int32)[None, :]).astype(F32)
-    hot = jnp.broadcast_to(hot.reshape(-1, 1), (2 * len(images), 128))
 
     parts = [item.T for item in affines]
     shards = list(filters)
@@ -1260,7 +1263,9 @@
         [Reduce.scratch(8, width, spare, k == LAST) for k, width in enumerate(rounds[0])],
         [Reduce.scratch(16, width // 2, spare, k == LAST, BF16) for k, width in enumerate(rounds[1])],
     ]
-    operands = dict(x=x, cot=cot, hot=hot, shards=shards)
+    operands = dict(x=x, cot=cot, shards=shards, views=[views_big, views_small])
+    anywhere, scalars = pl.BlockSpec(memory_space=pl.ANY), pl.BlockSpec(memory_space=pltpu.SMEM)
+    specs = dict(x=anywhere, cot=anywhere, shards=[anywhere] * len(shards), views=[scalars] * 2)
     results = dict(
         out=jax.ShapeDtypeStruct((half_rows, c_out), BF16),
         dinput=jax.ShapeDtypeStruct((full_rows, c_in), BF16),
@@ -1277,7 +1282,7 @@
         scale=[field(-(-len(images) // 8) * 8, width) for width in wide],
         x_v=rounded(full_rows, c_in),
         cot_v=rounded(half_rows, c_out),
-        hot_v=field(*hot.shape),
+        hot_v=field(2 * len(images), 128),
         cnt=field(8, 128),
         daffine_v=field(8, lane_total),
         F=field(max(full_rows, 4 * half_rows), c_in),
@@ -1320,7 +1325,7 @@
     flat_out = pl.pallas_call(
         kernel,
         out_shape=flat_out,
-        in_specs=[pl.BlockSpec(memory_space=pl.ANY)] * len(flat_in),
+        in_specs=jax.tree.leaves(specs),
         out_specs=[pl.BlockSpec(memory_space=pl.ANY)] * len(flat_out),
         scratch_shapes=flat_scratch,
         compiler_params=pltpu.CompilerParams(

time: 236 us -> 236 us (level)
  no operation moved by 1% of the time
where the time goes in v3:
time: 236 us; the launch traced here: 235 us
  Pallas kernels  219 us (93%)
  local copies, waits for them, and re-layouts  13.3 us (6%)
  other arithmetic  2.36 us (1%)
    pallas_call x1, Pallas kernels, local(): pl.pallas_call(kernel, out_shape=flat_out, in_specs=jax.tree.leaves(specs...  215 us
    unnamed x14, local copies, waits for them, and re-layouts  10.8 us

profile of v3, /device:TPU:1, one launch (start us, length us, event | category | flops | bytes accessed | tf_op | source)
XLA Modules:
  0.0 235.5 jit_solution(8810466280690650253)
XLA Ops:
  0.7 0.7 pad.26
  1.3 0.8 concatenate.10
  2.2 0.6 pad.27.flat_8_
  2.8 1.0 copy.47
  3.8 0.1 pad.25.clone
  3.8 0.0 copy-start.2
  3.8 1.2 copy.46
  5.0 0.1 pad.24.clone
  5.1 0.0 copy-start.1
  5.1 1.0 pad_maximum_fusion.1.flat_0_
  6.2 0.0 copy-done.2
  6.2 0.1 copy.49
  6.3 0.1 pad.29.clone
  6.4 0.1 copy-done.1
  6.6 0.2 copy.48
  6.8 0.1 pad.28.clone
  6.9 1.3 pad_maximum_fusion.flat_11_
  8.2 214.9 %shard_map.331 = (f32[8,6656]{1,0:T(8,128)}, bf16[64,256]{1,0:T(8,128)(2,1)}, bf16[144,256]{1,0:T(8,128)(2,1)}, bf16[16,1024]{1,0:T(8,128)(2,1)}, bf16[64,512]{1...) custom-call(bf16[224,2048]{1,0:T(8,128)(2,1)} %pad_maximum_fusion.1., ...), custom_call_target="tpu_custom_call" | custom-call | tf_op jit(solution)/shard_map/pallas_call | solution.py:1325
  223.1 4.2 %shard_map.332 = (bf16[2,7,7,2048]{3,2,1,0:T(8,128)(2,1)}, bf16[2,5,5,2048]{3,2,1,0:T(8,128)(2,1)}, bf16[2,14,14,1024]{3,2,1,0:T(8,128)(2,1)}, bf16[2,10,10,1024...) custom-call(bf16[224,2048]{1,0:T(8,128)(2,1)} %get-tuple-element.46., ...), custom_call_target="tpu_custom_call" | custom-call | tf_op jit(solution)/shard_map/pallas_call | solution.py:1374
  227.3 0.0 copy-start
  227.3 2.3 copy.42
  229.6 1.9 copy.43
  231.5 2.3 copy.45
  233.8 0.0 copy-done
  233.8 1.7 copy.44
  (1 shorter events, 0.0 us)
Async XLA Ops:
  3.8 2.4 %copy-start.2 = (bf16[2,10,10,1024]{3,0,2,1:T(2,128)(2,1)S(1)}, bf16[2,10,10,1024]{3,0,2,1:T(2,128)(2,1)}, u32[]{:S(2)}) copy-start(bf16[2,10,10,1024]{3,0,2,1:T(2,128)(2,1)} %param.21) | copy-start | bytes 1228804
  5.1 1.4 copy-start.1
  227.3 6.4 %copy-start = (bf16[2,14,14,1024]{3,2,1,0:T(8,128)(2,1)S(1)}, bf16[2,14,14,1024]{3,2,1,0:T(8,128)(2,1)}, u32[]{:S(2)}) copy-start(bf16[2,14,14,1024]{3,2,1,0:T(8,128)(2,1)} %get-tuple-element.76) | copy-start | bytes 2408452
